TPU v7x, 256 devices: a whole 4x4x8 slice. The times are simulated.
256 devices in a mesh: dp: 16 (over z_hi, x, core), tensor: 16 (over y, z_lo).
Axes of the slice: x: 4, y: 4, z: 8 (z_hi: 2, z_lo: 4; z = z_hi * 4 + z_lo), core: 2. Of those that a mesh axis runs over, the one named last changes fastest.
Arguments:
- gate_inputs: bfloat16 [4096, 30720], P('dp', 'tensor'), parts along dimension 0, may hold values from -6 to 6
- up_inputs: bfloat16 [4096, 30720], P('dp', 'tensor'), parts along dimension 0, may hold values from -6 to 6
- down_codes: float32 [5120, 8192], P('tensor'), may hold values from -8388608 to 8388607, as said below
- column_scale: float32 [8192], replicated, may hold values from 0.0008 to 0.004
Outputs:
- mixed: bfloat16 [4096, 8192], P(('dp', 'tensor')), parts along dimension 0
There are 16 independent parts, one for each index of `dp`. A program takes and returns all parts, laid end to end along the dimension named above; an argument that names none is the same for every part. Nothing has to cross between parts.
Inputs may be any that keep to these rules, and one draw needn't show every extreme that they name: `down_codes`: every entry is a whole number; the six base-16 digits of the entry plus 8388608 are independent 4-bit levels of six consecutive hidden units.
All inputs are finite; a program needn't handle non-finite values.
Results may differ from a plain program's by a relative error of at most 0.027.
Values may be sent and summed in bfloat16 or wider, within the bound.
A program may use at most 128 MiB of HBM per device.

v0:
```python
import math

import jax
import jax.numpy as jnp
from jax import lax
from jax.sharding import PartitionSpec as P


def from_partner(value, axis, apart):
    mask = 2**apart
    pairs = [(source, source ^ mask) for source in range(lax.axis_size(axis))]
    return lax.ppermute(value, axis, pairs)


def sylvester(extent):
    indices = jnp.arange(extent, dtype=jnp.int32)
    common = jnp.bitwise_and(indices[:, None], indices[None, :])
    parity = jnp.zeros((extent, extent), jnp.int32)
    for offset in range(extent.bit_length() - 1):
        parity = parity + jnp.bitwise_and(jnp.right_shift(common, offset), 1)
    return (1 - 2 * (parity % 2)).astype(jnp.float32)


def digit_planes(code_block):
    shifted = code_block.astype(jnp.int32) + 8388608
    plane_list = []
    for position in range(6):
        digit_value = jnp.bitwise_and(jnp.right_shift(shifted, 4 * position), 15) - 8
        plane_list.append(digit_value.astype(jnp.bfloat16))
    planes = jnp.stack(plane_list, axis=0)
    return planes.reshape(6 * code_block.shape[0], code_block.shape[1])


def body(gate_inputs, up_inputs, down_codes, column_scale):
    hidden = (jax.nn.silu(gate_inputs.astype(jnp.float32)) * up_inputs.astype(jnp.float32)).astype(
        jnp.bfloat16
    )
    row_total, hidden_width = hidden.shape
    shards = lax.axis_size("tensor")
    groups = hidden_width // 128
    scaling = 1.0 / math.sqrt(128 * shards)
    hadamard_local = sylvester(128)
    current = hidden.astype(jnp.float32)
    position = lax.axis_index("tensor")
    for level_bit in range(shards.bit_length() - 1):
        partner = from_partner(current.astype(jnp.bfloat16), "tensor", level_bit).astype(
            current.dtype
        )
        is_lower = jnp.bitwise_and(jnp.right_shift(position, level_bit), 1) == 0
        current = jnp.where(is_lower, current + partner, partner - current)
    turned = jnp.einsum(
        "rgj,kj->rgk",
        current.reshape(row_total, groups, 128),
        hadamard_local,
        precision=lax.Precision.HIGHEST,
    )
    rotated = (turned * scaling).astype(jnp.bfloat16).reshape(row_total, hidden_width)
    packed_rows = hidden_width // 6
    reordered = (
        rotated.reshape(row_total, packed_rows, 6)
        .transpose(0, 2, 1)
        .reshape(row_total, hidden_width)
    )
    levels = digit_planes(down_codes)
    return lax.psum_scatter(
        (jnp.dot(reordered, levels, preferred_element_type=jnp.float32) * column_scale).astype(
            jnp.bfloat16
        ),
        "tensor",
        scatter_dimension=0,
        tiled=True,
    )


def solution(mesh):
    return jax.shard_map(
        body,
        mesh=mesh,
        in_specs=(P("dp", "tensor"), P("dp", "tensor"), P("tensor", None), P()),
        out_specs=P(("dp", "tensor"), None),
        check_vma=False,
    )
```

profile of v0, /device:TPU:4, one launch (start us, length us, event | category | flops | bytes accessed | tf_op | source)
XLA Modules:
  0.0 271.6 jit_solution(12192077531577988376)
XLA Ops:
  6.5 0.0 reduce-scatter.2.cloned.1.call-start
  6.5 2.3 copy.8
  8.8 0.0 slice-start
  8.8 2.4 copy.7
  11.2 2.1 fusion.22
  13.3 0.0 slice-start.1
  13.3 0.0 slice-start.2
  13.3 2.0 collective-permute-start
  15.3 8.9 %fusion.3 = bf16[6,320,8192]{2,1,0:T(8,128)(2,1)} fusion(f32[320,8192]{1,0:T(8,128)} %param.6), kind=kLoop, calls=%fused_computation.11 | loop fusion | flops 15728639 | bytes 15728640
  24.2 0.0 slice-done
  24.2 0.0 slice-done.1
  24.3 0.0 slice-done.2
  24.3 4.9 %fusion.5 = bf16[6,320,8192]{2,1,0:T(8,128)(2,1)} fusion(bf16[6,320,8192]{2,1,0:T(8,128)(2,1)} %fusion.3, f32[320,8192]{1,0:T(8,128)S(1)} %bitcast.40), kind=kLoop, calls=%fused_computation.13 | loop fusion | flops 15728640 | bytes 15728640
  29.2 4.9 %fusion.7 = bf16[6,320,8192]{2,1,0:T(8,128)(2,1)} fusion(bf16[6,320,8192]{2,1,0:T(8,128)(2,1)} %fusion.5, f32[320,8192]{1,0:T(8,128)S(1)} %bitcast.40), kind=kLoop, calls=%fused_computation.15 | loop fusion | flops 15728640 | bytes 15728640
  34.1 3.1 %collective-permute-done = bf16[256,1920]{0,1:T(8,128)(2,1)} collective-permute-done((bf16[256,1920]{0,1:T(8,128)(2,1)S(1)}, bf16[256,1920]{0,1:T(8,128)(2,1)}, u32[]{:S(2)}, u32[]{:S(2)}) %collective-permute-start) | collective-permute-done | bytes 983072 | tf_op jit(solution)/shard_map/ppermute | solution.py:12
  37.2 1.6 fusion.23
  38.8 3.5 %collective-permute-start.1 = (bf16[256,1920]{0,1:T(8,128)(2,1)S(1)}, bf16[256,1920]{0,1:T(8,128)(2,1)S(1)}, u32[]{:S(2)}, u32[]{:S(2)}) collective-permute-start(bf16[256,1920]{0,1:T(8,128)(2,1)S(1)} %fusion.23), channel_id=1, source_target_pairs={{0,2},{1,3},{2,0},{3,1},{4,6},{5,7},{6,4},{7,5},{8,10},{9,11},{10,... | collective-permute-start | bytes 2949128 | tf_op jit(solution)/shard_map/ppermute | solution.py:12
  42.3 8.8 %fusion.9 = bf16[6,320,8192]{2,1,0:T(8,128)(2,1)} fusion(bf16[6,320,8192]{2,1,0:T(8,128)(2,1)} %fusion.7, f32[320,8192]{1,0:T(8,128)} %param.6), kind=kLoop, calls=%fused_computation.17 | loop fusion | flops 15728640 | bytes 15728640
  51.1 33.3 %collective-permute-done.1 = bf16[256,1920]{0,1:T(8,128)(2,1)S(1)} collective-permute-done((bf16[256,1920]{0,1:T(8,128)(2,1)S(1)}, bf16[256,1920]{0,1:T(8,128)(2,1)S(1)}, u32[]{:S(2)}, u32[]{:S(2)}) %collective-permute-start.1) | collective-permute-done | bytes 983072 | tf_op jit(solution)/shard_map/ppermute | solution.py:12
  84.4 2.8 %fusion.49 = bf16[256,1920]{0,1:T(8,128)(2,1)} fusion(bf16[256,1920]{0,1:T(8,128)(2,1)S(1)} %collective-permute-done.1, bf16[256,1920]{0,1:T(8,128)(2,1)} %collective-permute-done, bf16[256,1920]{0,1:T(8,128)(2,1)S(1)} %fusion.22, pred[]{:T(512)S(6)} %eq.17, pred[]{:T(512)S(6)} %eq.16), kind=kLoop, calls=%fused_computation.70 | loop fusion | flops 4915200 | bytes 3932162 | tf_op jit(solution)/shard_map/convert_element_type | solution.py:46
  87.2 1.6 collective-permute-start.2
  88.8 8.9 %fusion.11 = bf16[6,320,8192]{2,1,0:T(8,128)(2,1)} fusion(bf16[6,320,8192]{2,1,0:T(8,128)(2,1)} %fusion.9, f32[320,8192]{1,0:T(8,128)} %param.6), kind=kLoop, calls=%fused_computation.19 | loop fusion | flops 15728640 | bytes 15728640
  97.7 12.4 %collective-permute-done.2 = bf16[256,1920]{0,1:T(8,128)(2,1)S(1)} collective-permute-done((bf16[256,1920]{0,1:T(8,128)(2,1)}, bf16[256,1920]{0,1:T(8,128)(2,1)S(1)}, u32[]{:S(2)}, u32[]{:S(2)}) %collective-permute-start.2) | collective-permute-done | bytes 983072 | tf_op jit(solution)/shard_map/ppermute | solution.py:12
  110.1 3.0 %fusion.24 = bf16[256,1920]{0,1:T(8,128)(2,1)} fusion(bf16[256,1920]{0,1:T(8,128)(2,1)S(1)} %collective-permute-done.2, pred[]{:T(512)S(6)} %eq.15, bf16[256,1920]{0,1:T(8,128)(2,1)S(1)} %collective-permute-done.1, bf16[256,1920]{0,1:T(8,128)(2,1)} %collective-permute-done, bf16[256,1920]{0,1:T(8,128)(2,1)S(1)} %fusion.22, pred[]{:T(512)S(6)} %eq.17, pred[]{:T(512)S(6)} %eq.16), kind=kLoop, calls=%fused_computation.43 | loop fusion | flops 6881280 | bytes 4915203 | tf_op jit(solution)/shard_map/convert_element_type | solution.py:46
  113.1 0.0 copy-start
  113.1 3.2 %collective-permute-start.3 = (bf16[256,1920]{0,1:T(8,128)(2,1)}, bf16[256,1920]{0,1:T(8,128)(2,1)}, u32[]{:S(2)}, u32[]{:S(2)}) collective-permute-start(bf16[256,1920]{0,1:T(8,128)(2,1)} %fusion.24), channel_id=1, source_target_pairs={{0,8},{1,9},{2,10},{3,11},{4,12},{5,13},{6,14},{7,15},{8,0},{9,1},... | collective-permute-start | bytes 2949128 | tf_op jit(solution)/shard_map/ppermute | solution.py:12
  116.3 8.9 %fusion.13 = bf16[6,320,8192]{2,1,0:T(8,128)(2,1)} fusion(bf16[6,320,8192]{2,1,0:T(8,128)(2,1)} %fusion.11, f32[320,8192]{1,0:T(8,128)} %param.6), kind=kLoop, calls=%fused_computation.21 | loop fusion | flops 15728640 | bytes 15728640 | tf_op jit(solution)/shard_map/stack | solution.py:30
  125.2 11.4 %collective-permute-done.3 = bf16[256,1920]{0,1:T(8,128)(2,1)} collective-permute-done((bf16[256,1920]{0,1:T(8,128)(2,1)}, bf16[256,1920]{0,1:T(8,128)(2,1)}, u32[]{:S(2)}, u32[]{:S(2)}) %collective-permute-start.3) | collective-permute-done | bytes 983072 | tf_op jit(solution)/shard_map/ppermute | solution.py:12
  136.6 2.6 fusion.21
  139.2 2.0 multiply_convert_fusion
  141.2 0.4 reshape_reshape.3
  141.6 0.0 copy-done
  141.6 16.4 %fusion.1 = bf16[256,8192]{1,0:T(8,128)(2,1)} fusion(bf16[6,320,8192]{2,1,0:T(8,128)(2,1)} %fusion.13, f32[8192]{0:T(1024)S(1)} %copy-done, bf16[256,6,320]{0,1,2:T(8,128)(2,1)S(1)} %bitcast.42), kind=kOutput, calls=%fused_computation.9 | convolution fusion | flops 8057257984 | bytes 36667392 | tf_op jit(solution)/shard_map/dot_general | solution.py:66
  158.0 0.0 reduce-scatter.2.cloned.1.call-update
  158.0 106.7 %reduce-scatter.2.cloned.1.call-done = bf16[16,8192]{1,0:T(8,128)(2,1)} async-done(((bf16[256,8192]{1,0:T(8,128)(2,1)}), bf16[16,8192]{1,0:T(8,128)(2,1)}) %reduce-scatter.2.cloned.1.call-update) | async-done | bytes 262160 | tf_op jit(solution)/shard_map/reduce_scatter | solution.py:65
  (1 shorter events, 0.0 us)
Async XLA Ops:
  6.5 258.2 %reduce-scatter.2.cloned.1.call-start = ((), (), s32[]{:S(2)}) async-start(), calls=%async_computation.1 | async-start | bytes 4456448 | tf_op jit(solution)/shard_map/reduce_scatter | solution.py:65
  8.8 15.4 %slice-start = ((s8[10485760]{0:T(1024)(128)(4,1)}), s8[2097152]{0:T(1024)(128)(4,1)S(1)}, s32[]{:S(2)}) async-start(s8[10485760]{0:T(1024)(128)(4,1)} %bitcast.39), calls=%async_computation.2 | async-start | bytes 4194304
  13.3 10.9 %slice-start.1 = ((s8[10485760]{0:T(1024)(128)(4,1)}), s8[4194304]{0:T(1024)(128)(4,1)S(1)}, s32[]{:S(2)}) async-start(s8[10485760]{0:T(1024)(128)(4,1)} %bitcast.39), calls=%async_computation.3 | async-start | bytes 8388608
  13.3 10.9 %slice-start.2 = ((s8[10485760]{0:T(1024)(128)(4,1)}), s8[4194304]{0:T(1024)(128)(4,1)S(1)}, s32[]{:S(2)}) async-start(s8[10485760]{0:T(1024)(128)(4,1)} %bitcast.39), calls=%async_computation.4 | async-start | bytes 8388608
  13.3 23.9 %collective-permute-start = (bf16[256,1920]{0,1:T(8,128)(2,1)S(1)}, bf16[256,1920]{0,1:T(8,128)(2,1)}, u32[]{:S(2)}, u32[]{:S(2)}) collective-permute-start(bf16[256,1920]{0,1:T(8,128)(2,1)S(1)} %fusion.22), channel_id=1, source_target_pairs={{0,1},{1,0},{2,3},{3,2},{4,5},{5,4},{6,7},{7,6},{8,9},{9,8},{10,11... | collective-permute-start | bytes 2949128 | tf_op jit(solution)/shard_map/ppermute | solution.py:12
  38.8 45.7 %collective-permute-start.1 = (bf16[256,1920]{0,1:T(8,128)(2,1)S(1)}, bf16[256,1920]{0,1:T(8,128)(2,1)S(1)}, u32[]{:S(2)}, u32[]{:S(2)}) collective-permute-start(bf16[256,1920]{0,1:T(8,128)(2,1)S(1)} %fusion.23), channel_id=1, source_target_pairs={{0,2},{1,3},{2,0},{3,1},{4,6},{5,7},{6,4},{7,5},{8,10},{9,11},{10,... | collective-permute-start | bytes 2949128 | tf_op jit(solution)/shard_map/ppermute | solution.py:12
  87.2 22.8 %collective-permute-start.2 = (bf16[256,1920]{0,1:T(8,128)(2,1)}, bf16[256,1920]{0,1:T(8,128)(2,1)S(1)}, u32[]{:S(2)}, u32[]{:S(2)}) collective-permute-start(bf16[256,1920]{0,1:T(8,128)(2,1)} %fusion.49), channel_id=1, source_target_pairs={{0,4},{1,5},{2,6},{3,7},{4,0},{5,1},{6,2},{7,3},{8,12},{9,13},{10,... | collective-permute-start | bytes 2949128 | tf_op jit(solution)/shard_map/ppermute | solution.py:12
  113.1 28.5 %copy-start = (f32[8192]{0:T(1024)S(1)}, f32[8192]{0:T(1024)}, u32[]{:S(2)}) copy-start(f32[8192]{0:T(1024)} %param.7) | copy-start | bytes 98308
  113.1 23.5 %collective-permute-start.3 = (bf16[256,1920]{0,1:T(8,128)(2,1)}, bf16[256,1920]{0,1:T(8,128)(2,1)}, u32[]{:S(2)}, u32[]{:S(2)}) collective-permute-start(bf16[256,1920]{0,1:T(8,128)(2,1)} %fusion.24), channel_id=1, source_target_pairs={{0,8},{1,9},{2,10},{3,11},{4,12},{5,13},{6,14},{7,15},{8,0},{9,1},... | collective-permute-start | bytes 2949128 | tf_op jit(solution)/shard_map/ppermute | solution.py:12
Sparse Core Ops, SparseCore 0:
  158.1 106.5 reduce-scatter.1
where the time goes:
time: 272 us
  waiting for transfers between devices  167 us (61%)
  other arithmetic  57.4 us (21%)
  matrix products  18.4 us (7%)
  between operations  13.5 us (5%)
  starting transfers between devices  10.3 us (4%)
  local copies, waits for them, and re-layouts  5.06 us (2%)
    reduce_scatter x1, waiting for transfers between devices, body(): lax.psum_scatter((jnp.dot(reordered, levels, preferred_element_type=jnp.f...  107 us
    ppermute x4, waiting for transfers between devices, from_partner(): return lax.ppermute(value, axis, pairs)  60.2 us
    unnamed x6, other arithmetic  36.4 us
    dot_general x1, matrix products, body(): jnp.dot(reordered, levels, preferred_element_type=jnp.float32)  16.4 us
    ppermute x4, starting transfers between devices, from_partner(): return lax.ppermute(value, axis, pairs)  10.3 us
    another operation x1, other arithmetic, digit_planes(): planes = jnp.stack(plane_list, axis=0)  8.93 us
    convert_element_type x3, other arithmetic, body(): current.astype(jnp.bfloat16)  7.35 us
  transfers between devices with their start and end apart: 5, of which 5 were waited for; matrix products, arithmetic and copies ran while one was open for 17% of the time, Pallas kernels for 0%

commit v1 on v0

v1 whole, which is shorter than its diff:
```python
import functools
import math

import jax
import jax.numpy as jnp
import ml_dtypes
import numpy as np
from jax import lax
from jax.experimental import pallas as pl
from jax.experimental.pallas import tpu as pltpu
from jax.sharding import PartitionSpec as P

MESH = pl.DeviceIdType.MESH
NY, NZ, RUN = 4, 8, 4
SHARDS = NY * RUN
SUPER = 384
CODE_ROWS = SUPER // 6
LAG_B, LAG_C, LAG_D = 2, 4, 6


def sylvester(extent):
    indices = np.arange(extent)
    common = indices[:, None] & indices[None, :]
    parity = np.zeros((extent, extent), np.int64)
    for offset in range(extent.bit_length() - 1):
        parity += (common >> offset) & 1
    return 1 - 2 * (parity % 2)


def turn_matrix():
    blocks = np.kron(np.eye(SUPER // 128), sylvester(128))
    order = np.arange(SUPER).reshape(CODE_ROWS, 6).T.reshape(-1)
    return blocks[:, order].astype(ml_dtypes.bfloat16)


def kernel(
    half,
    width,
    gate_hbm,
    up_hbm,
    codes_hbm,
    scale_ref,
    turn_ref,
    out_ref,
    gate,
    up,
    codes,
    hidden,
    gathered,
    turned,
    rot,
    levels,
    part,
    from_below_a,
    from_above_a,
    from_below_b,
    from_above_b,
    from_z,
    load_sem,
    code_sem,
    gather_send,
    gather_recv,
    scatter_send,
    scatter_recv,
    a_send,
    a_recv,
    b_send,
    b_recv,
    z_send,
    z_recv,
):
    rows, hidden_width = gate.shape
    features = levels.shape[1]
    supers = hidden_width // SUPER
    piece = rows // SHARDS
    block = rows // NY
    chunks = features // width
    dp = lax.axis_index("dp")
    me = lax.axis_index("tensor")
    rest = lax.rem(dp, half)
    y = lax.div(me, RUN)
    z_lo = lax.rem(me, RUN)
    z = lax.div(dp, half) * RUN + z_lo
    z_far = lax.rem(z + 6 - 4 * lax.div(z_lo, 2), NZ)
    z_of = (z, lax.rem(z + 1, NZ), lax.rem(z + NZ - 1, NZ), z_far)
    slot_there = (0, 2, 1, 3)

    def device(y_there, z_there):
        return (lax.div(z_there, RUN) * half + rest, y_there * RUN + lax.rem(z_there, RUN))

    def y_of(apart):
        return lax.rem(y + apart, NY)

    def wait_for(ref, sem):
        pltpu.make_async_copy(ref, ref, sem).wait()

    def send(src, dst, send_sem, recv_sem, where):
        pltpu.make_async_remote_copy(
            src_ref=src, dst_ref=dst, send_sem=send_sem, recv_sem=recv_sem, device_id=where, device_id_type=MESH
        ).start()

    barrier = pltpu.get_barrier_semaphore()

    def greet(apart, carry):
        pl.semaphore_signal(barrier, inc=1, device_id=(dp, lax.rem(me + apart, SHARDS)), device_id_type=MESH)
        return carry

    load_gate = pltpu.make_async_copy(gate_hbm, gate, load_sem.at[0])
    load_up = pltpu.make_async_copy(up_hbm, up, load_sem.at[1])
    load_gate.start()
    load_up.start()
    lax.fori_loop(1, SHARDS, greet, 0)
    for slot in (1, 2, 3):

        @pl.when(lax.div(z_of[slot], RUN) != lax.div(z, RUN))
        def _(slot=slot):
            def greet_across(apart, carry):
                pl.semaphore_signal(
                    barrier, inc=1, device_id=device(y_of(apart), z_of[slot]), device_id_type=MESH
                )
                return carry

            lax.fori_loop(0, NY, greet_across, 0)

    def code_copy(q):
        span = pl.ds(pl.multiple_of(q * CODE_ROWS, CODE_ROWS), CODE_ROWS)
        return pltpu.make_async_copy(codes_hbm.at[span, :], codes.at[span, :], code_sem.at[q])

    for q in range(supers):
        code_copy(q).start()
    load_gate.wait()
    load_up.wait()
    across = 1 + lax.rem(lax.div(z_lo + 1, 2) + 1, 2)
    pl.semaphore_wait(barrier, SHARDS - 1 + NY * across)

    def send_hidden(q, carry):
        span = pl.ds(pl.multiple_of(q * SUPER, 128), SUPER)

        def hidden_of(owner):
            its = pl.ds(pl.multiple_of(owner * piece, piece), piece)
            g = gate[its, span].astype(jnp.float32)
            value = g / (1.0 + jnp.exp(-g)) * up[its, span].astype(jnp.float32)
            return its, value.astype(jnp.bfloat16)

        mine = pl.ds(pl.multiple_of(me * piece, piece), piece)
        for apart in range(1, SHARDS):
            owner = lax.rem(me + apart, SHARDS)
            its, value = hidden_of(owner)
            hidden[its, span] = value
            send(
                hidden.at[its, span], gathered.at[mine, span], gather_send, gather_recv.at[q], (dp, owner)
            )
        its, value = hidden_of(me)
        gathered[its, span] = value
        return carry

    lax.fori_loop(0, supers, send_hidden, 0)

    def rotate(q, carry):
        span = pl.ds(pl.multiple_of(q * SUPER, 128), SUPER)
        code_copy(q).wait()

        def decode(tile, inner):
            columns = pl.ds(pl.multiple_of(tile * 256, 256), 256)
            code_span = pl.ds(pl.multiple_of(q * CODE_ROWS, CODE_ROWS), CODE_ROWS)
            shifted = codes[code_span, columns].astype(jnp.int32) + 8388608
            for digit in range(6):
                value = jnp.bitwise_and(jnp.right_shift(shifted, 4 * digit), 15) - 8
                level_span = pl.ds(pl.multiple_of(q * SUPER + digit * CODE_ROWS, CODE_ROWS), CODE_ROWS)
                levels[level_span, columns] = value.astype(jnp.float32).astype(jnp.bfloat16)
            return inner

        lax.fori_loop(0, features // 256, decode, 0)
        wait_for(gathered.at[pl.ds(0, (SHARDS - 1) * piece), span], gather_recv.at[q])
        local = jnp.dot(gathered[:, span], turn_ref[...], preferred_element_type=jnp.float32)
        terms = [local[piece * t : piece * (t + 1)] for t in range(SHARDS)]
        step = 1
        while step < SHARDS:
            after = list(terms)
            for t in range(SHARDS):
                if not t & step:
                    after[t] = terms[t] + terms[t + step]
                    after[t + step] = terms[t] - terms[t + step]
            terms, step = after, 2 * step
        scaling = 1.0 / math.sqrt(128 * SHARDS)
        for t in range(SHARDS):
            turned[piece * t : piece * (t + 1), span] = (terms[t] * scaling).astype(jnp.bfloat16)
        for slot in (3, 1, 2, 0):
            for apart in (2, 1, 3, 0):
                if slot == 0 and apart == 0:
                    continue
                shard = y_of(apart) * RUN + lax.rem(z_of[slot], RUN)
                row = (((NY - apart) % NY) * 4 + slot_there[slot]) * piece
                send(
                    turned.at[pl.ds(pl.multiple_of(shard * piece, piece), piece), span],
                    rot.at[pl.ds(row, piece), span],
                    scatter_send,
                    scatter_recv.at[q],
                    device(y_of(apart), z_of[slot]),
                )
        rot[0:piece, span] = turned[pl.ds(pl.multiple_of(me * piece, piece), piece), span]
        return carry

    lax.fori_loop(0, supers, rotate, 0)

    def wait_rotated(q, carry):
        span = pl.ds(pl.multiple_of(q * SUPER, 128), SUPER)
        wait_for(rot.at[pl.ds(0, (SHARDS - 1) * piece), span], scatter_recv.at[q])
        return carry

    lax.fori_loop(0, supers, wait_rotated, 0)

    def columns_of(c):
        return pl.ds(pl.multiple_of(c * width, width), width)

    def half_of(c):
        return pl.ds(pl.multiple_of(c * (width // 2), width // 2), width // 2)

    def lower_of(c):
        return pl.ds(pl.multiple_of(c * width, width // 2), width // 2)

    def upper_of(c):
        return pl.ds(pl.multiple_of(c * width + width // 2, width // 2), width // 2)

    def added(*values):
        total = values[0].astype(jnp.float32)
        for value in values[1:]:
            total = total + value.astype(jnp.float32)
        return total.astype(jnp.bfloat16)

    above, below = device(y_of(1), z), device(y_of(NY - 1), z)
    own, next_y, opposite, last_y = (pl.ds(block * i, block) for i in range(NY))

    def step(t, carry):
        @pl.when(t < chunks)
        def _():
            c = t
            product = jnp.dot(rot[...], levels[:, columns_of(c)], preferred_element_type=jnp.float32)
            part[:, columns_of(c)] = (product * scale_ref[:, columns_of(c)]).astype(jnp.bfloat16)
            send(part.at[opposite, lower_of(c)], from_below_a.at[:, half_of(c)], a_send, a_recv.at[0, c], above)
            send(part.at[opposite, upper_of(c)], from_above_a.at[:, half_of(c)], a_send, a_recv.at[1, c], below)

        @pl.when((t >= LAG_B) & (t < chunks + LAG_B))
        def _():
            c = t - LAG_B
            wait_for(from_below_a.at[:, half_of(c)], a_recv.at[0, c])
            part[next_y, lower_of(c)] = added(part[next_y, lower_of(c)], from_below_a[:, half_of(c)])
            send(part.at[next_y, columns_of(c)], from_below_b.at[:, columns_of(c)], b_send, b_recv.at[0, c], above)
            wait_for(from_above_a.at[:, half_of(c)], a_recv.at[1, c])
            part[last_y, upper_of(c)] = added(part[last_y, upper_of(c)], from_above_a[:, half_of(c)])
            send(part.at[last_y, columns_of(c)], from_above_b.at[:, columns_of(c)], b_send, b_recv.at[1, c], below)

        @pl.when((t >= LAG_C) & (t < chunks + LAG_C))
        def _():
            c = t - LAG_C
            wait_for(from_below_b.at[:, columns_of(c)], b_recv.at[0, c])
            wait_for(from_above_b.at[:, columns_of(c)], b_recv.at[1, c])
            part[own, columns_of(c)] = added(
                part[own, columns_of(c)], from_below_b[:, columns_of(c)], from_above_b[:, columns_of(c)]
            )
            for slot in (3, 1, 2):
                send(
                    part.at[pl.ds(slot * piece, piece), columns_of(c)],
                    from_z.at[pl.ds((slot_there[slot] - 1) * piece, piece), columns_of(c)],
                    z_send,
                    z_recv.at[slot_there[slot] - 1, c],
                    device(y, z_of[slot]),
                )

        @pl.when(t >= LAG_D)
        def _():
            c = t - LAG_D
            for slot in range(3):
                wait_for(from_z.at[pl.ds(slot * piece, piece), columns_of(c)], z_recv.at[slot, c])
            out_ref[:, columns_of(c)] = added(
                part[pl.ds(0, piece), columns_of(c)],
                *(from_z[pl.ds(slot * piece, piece), columns_of(c)] for slot in range(3)),
            )

        return carry

    lax.fori_loop(0, chunks + LAG_D, step, 0)

    wait_for(gathered.at[pl.ds(0, (SHARDS - 1) * piece), :], gather_send)
    wait_for(rot.at[pl.ds(0, (SHARDS - 1) * piece), :], scatter_send)
    wait_for(part.at[opposite, :], a_send)
    wait_for(part.at[pl.ds(0, 2 * block), :], b_send)
    wait_for(from_z, z_send)


def body(gate_inputs, up_inputs, down_codes, column_scale, half):
    rows, hidden_width = gate_inputs.shape
    code_rows, features = down_codes.shape
    width = min(512, features // 2)
    chunks = features // width
    supers = hidden_width // SUPER
    piece, block = rows // SHARDS, rows // NY
    whole = pl.BlockSpec(memory_space=pltpu.VMEM)
    outside = pl.BlockSpec(memory_space=pl.ANY)
    b16 = jnp.bfloat16
    return pl.pallas_call(
        functools.partial(kernel, half, width),
        out_shape=jax.ShapeDtypeStruct((piece, features), b16),
        in_specs=[outside, outside, outside, whole, whole],
        out_specs=whole,
        scratch_shapes=[
            pltpu.VMEM((rows, hidden_width), b16),
            pltpu.VMEM((rows, hidden_width), b16),
            pltpu.VMEM((code_rows, features), jnp.float32),
            pltpu.VMEM((rows, hidden_width), b16),
            pltpu.VMEM((rows, hidden_width), b16),
            pltpu.VMEM((rows, hidden_width), b16),
            pltpu.VMEM((rows, hidden_width), b16),
            pltpu.VMEM((hidden_width, features), b16),
            pltpu.VMEM((rows, features), b16),
            pltpu.VMEM((block, features // 2), b16),
            pltpu.VMEM((block, features // 2), b16),
            pltpu.VMEM((block, features), b16),
            pltpu.VMEM((block, features), b16),
            pltpu.VMEM((3 * piece, features), b16),
            pltpu.SemaphoreType.DMA((2,)),
            pltpu.SemaphoreType.DMA((supers,)),
            pltpu.SemaphoreType.DMA,
            pltpu.SemaphoreType.DMA((supers,)),
            pltpu.SemaphoreType.DMA,
            pltpu.SemaphoreType.DMA((supers,)),
            pltpu.SemaphoreType.DMA,
            pltpu.SemaphoreType.DMA((2, chunks)),
            pltpu.SemaphoreType.DMA,
            pltpu.SemaphoreType.DMA((2, chunks)),
            pltpu.SemaphoreType.DMA,
            pltpu.SemaphoreType.DMA((3, chunks)),
        ],
        compiler_params=pltpu.CompilerParams(
            collective_id=0, has_side_effects=True, vmem_limit_bytes=60 * 1024 * 1024
        ),
    )(gate_inputs, up_inputs, down_codes, column_scale.reshape(1, features), jnp.asarray(turn_matrix()))


def solution(mesh):
    return jax.shard_map(
        functools.partial(body, half=mesh.shape["dp"] // 2),
        mesh=mesh,
        in_specs=(P("dp", "tensor"), P("dp", "tensor"), P("tensor", None), P()),
        out_specs=P(("dp", "tensor"), None),
        check_vma=False,
    )
```

time: 272 us -> 85.7 us (0.32)
  waiting for transfers between devices: 167 us -> 0 us
  Pallas kernels: 0 us -> 83.8 us
  other arithmetic: 57.4 us -> 0 us
  matrix products: 18.4 us -> 0 us
  between operations: 13.5 us -> 0.01 us
  starting transfers between devices: 10.3 us -> 0 us
  local copies, waits for them, and re-layouts: 5.06 us -> 1.67 us
    reduce_scatter x1 -> x0, waiting for transfers between devices: 107 us -> none  [body(): lax.psum_scatter((jnp.dot(reordered, levels, preferred_element_type=jnp.f...]
    pallas_call x0 -> x1, Pallas kernels: none -> 83.8 us  [body(): pl.pallas_call(functools.partial(kernel, half, width), out_shape=jax.Shap...]
    ppermute x4 -> x0, waiting for transfers between devices: 60.2 us -> none  [from_partner(): return lax.ppermute(value, axis, pairs)]
    unnamed x6 -> x0, other arithmetic: 36.4 us -> none
    dot_general x2 -> x0, matrix products: 18.4 us -> none  [the longest x1 16.4 us: body(): jnp.dot(reordered, levels, preferred_element_type=jnp.float32)]
    ppermute x4 -> x0, starting transfers between devices: 10.3 us -> none  [from_partner(): return lax.ppermute(value, axis, pairs)]
    convert_element_type x4 -> x0, other arithmetic: 9.45 us -> none  [the longest x3 7.35 us: body(): current.astype(jnp.bfloat16)]
    another operation x1 -> x0, other arithmetic: 8.93 us -> none  [digit_planes(): planes = jnp.stack(plane_list, axis=0)]
  transfers between devices with their start and end apart: 5 -> 0, of which waited for: 5 -> 0; matrix products, arithmetic and copies ran while one was open for 17% -> 0% of each run, Pallas kernels for 0% -> 0%
where the time goes in v1:
time: 85.7 us; the launch traced here: 85.5 us
  Pallas kernels  83.8 us (98%)
  local copies, waits for them, and re-layouts  1.67 us (2%)
    pallas_call x1, Pallas kernels, body(): pl.pallas_call(functools.partial(kernel, half, width), out_shape=jax.Shap...  83.8 us

profile of v1, /device:TPU:4, one launch (start us, length us, event | category | flops | bytes accessed | tf_op | source)
XLA Modules:
  0.0 85.5 jit_solution(5743322697638559422)
XLA Ops:
  0.0 83.8 %shard_map.55 = bf16[16,8192]{1,0:T(8,128)(2,1)} custom-call(bf16[256,1920]{1,0:T(8,128)(2,1)} %gate_hbm.1, bf16[256,1920]{1,0:T(8,128)(2,1)} %up_hbm.1, f32[320,8192]{1,0:T(8,128)} %codes_hbm.1, f32[1,8192]{1,0:T(1,128)} %bitcast.1, bf16[384,384]{1,0:T(8,128)(2,1)} %constant.2.clone.turn_ref), custom_call_target="tpu_custom_call" | custom-call | tf_op jit(solution)/shard_map/pallas_call | solution.py:301
  83.9 1.7 %copy.7 = bf16[16,8192]{1,0:T(8,128)(2,1)} copy(bf16[16,8192]{1,0:T(8,128)(2,1)} %shard_map.55) | data formatting | bytes 524288

commit v2 on v1

--- a/solution.py
+++ b/solution.py
@@ -15,7 +15,12 @@
 SHARDS = NY * RUN
 SUPER = 384
 CODE_ROWS = SUPER // 6
-LAG_B, LAG_C, LAG_D = 2, 4, 6
+PATTERN = ((384, 128), (384, 128), (384, 128), (256, 256))
+PERIOD = len(PATTERN)
+WIDTH = sum(PATTERN[0])
+FIRST = 2
+Z_SPAN = sum(z_width for _, z_width in PATTERN)
+LAG_B, LAG_C, LAG_D = 6, 10, 14
 
 
 def sylvester(extent):
@@ -35,13 +40,14 @@
 
 def kernel(
     half,
-    width,
     gate_hbm,
     up_hbm,
     codes_hbm,
-    scale_ref,
-    turn_ref,
+    scale_hbm,
+    turn_hbm,
     out_ref,
+    scale,
+    turn,
     gate,
     up,
     codes,
@@ -50,12 +56,15 @@
     turned,
     rot,
     levels,
+    first,
     part,
     from_below_a,
     from_above_a,
+    far_below,
+    far_above,
     from_below_b,
     from_above_b,
-    from_z,
+    from_owners,
     load_sem,
     code_sem,
     gather_send,
@@ -66,15 +75,14 @@
     a_recv,
     b_send,
     b_recv,
-    z_send,
-    z_recv,
+    c_send,
+    c_recv,
 ):
     rows, hidden_width = gate.shape
     features = levels.shape[1]
     supers = hidden_width // SUPER
     piece = rows // SHARDS
-    block = rows // NY
-    chunks = features // width
+    chunks = features // WIDTH
     dp = lax.axis_index("dp")
     me = lax.axis_index("tensor")
     rest = lax.rem(dp, half)
@@ -105,10 +113,20 @@
         pl.semaphore_signal(barrier, inc=1, device_id=(dp, lax.rem(me + apart, SHARDS)), device_id_type=MESH)
         return carry
 
-    load_gate = pltpu.make_async_copy(gate_hbm, gate, load_sem.at[0])
-    load_up = pltpu.make_async_copy(up_hbm, up, load_sem.at[1])
-    load_gate.start()
-    load_up.start()
+    def input_copies(q):
+        span = pl.ds(pl.multiple_of(q * SUPER, 128), SUPER)
+        return (
+            pltpu.make_async_copy(gate_hbm.at[:, span], gate.at[:, span], load_sem.at[0, q]),
+            pltpu.make_async_copy(up_hbm.at[:, span], up.at[:, span], load_sem.at[1, q]),
+        )
+
+    for q in range(supers):
+        for copy in input_copies(q):
+            copy.start()
+    load_turn = pltpu.make_async_copy(turn_hbm, turn, load_sem.at[2, 0])
+    load_scale = pltpu.make_async_copy(scale_hbm, scale, load_sem.at[2, 1])
+    load_turn.start()
+    load_scale.start()
     lax.fori_loop(1, SHARDS, greet, 0)
     for slot in (1, 2, 3):
 
@@ -126,15 +144,13 @@
         span = pl.ds(pl.multiple_of(q * CODE_ROWS, CODE_ROWS), CODE_ROWS)
         return pltpu.make_async_copy(codes_hbm.at[span, :], codes.at[span, :], code_sem.at[q])
 
-    for q in range(supers):
-        code_copy(q).start()
-    load_gate.wait()
-    load_up.wait()
     across = 1 + lax.rem(lax.div(z_lo + 1, 2) + 1, 2)
     pl.semaphore_wait(barrier, SHARDS - 1 + NY * across)
 
     def send_hidden(q, carry):
         span = pl.ds(pl.multiple_of(q * SUPER, 128), SUPER)
+        for copy in input_copies(q):
+            copy.wait()
 
         def hidden_of(owner):
             its = pl.ds(pl.multiple_of(owner * piece, piece), piece)
@@ -155,9 +171,12 @@
         return carry
 
     lax.fori_loop(0, supers, send_hidden, 0)
-
-    def rotate(q, carry):
-        span = pl.ds(pl.multiple_of(q * SUPER, 128), SUPER)
+    for q in range(supers):
+        code_copy(q).start()
+    load_turn.wait()
+    load_scale.wait()
+
+    def decode_levels(q):
         code_copy(q).wait()
 
         def decode(tile, inner):
@@ -171,8 +190,12 @@
             return inner
 
         lax.fori_loop(0, features // 256, decode, 0)
+
+    def rotate(q, carry):
+        span = pl.ds(pl.multiple_of(q * SUPER, 128), SUPER)
+        pl.when(q < supers - 1)(lambda: decode_levels(q))
         wait_for(gathered.at[pl.ds(0, (SHARDS - 1) * piece), span], gather_recv.at[q])
-        local = jnp.dot(gathered[:, span], turn_ref[...], preferred_element_type=jnp.float32)
+        local = jnp.dot(gathered[:, span], turn[...], preferred_element_type=jnp.float32)
         terms = [local[piece * t : piece * (t + 1)] for t in range(SHARDS)]
         step = 1
         while step < SHARDS:
@@ -202,25 +225,33 @@
         return carry
 
     lax.fori_loop(0, supers, rotate, 0)
+    decode_levels(supers - 1)
 
     def wait_rotated(q, carry):
         span = pl.ds(pl.multiple_of(q * SUPER, 128), SUPER)
         wait_for(rot.at[pl.ds(0, (SHARDS - 1) * piece), span], scatter_recv.at[q])
+        first[...] += jnp.dot(
+            rot[:, span], levels[span, 0 : FIRST * WIDTH], preferred_element_type=jnp.float32
+        )
         return carry
 
+    first[...] = jnp.zeros_like(first)
     lax.fori_loop(0, supers, wait_rotated, 0)
 
-    def columns_of(c):
-        return pl.ds(pl.multiple_of(c * width, width), width)
-
-    def half_of(c):
-        return pl.ds(pl.multiple_of(c * (width // 2), width // 2), width // 2)
-
-    def lower_of(c):
-        return pl.ds(pl.multiple_of(c * width, width // 2), width // 2)
-
-    def upper_of(c):
-        return pl.ds(pl.multiple_of(c * width + width // 2, width // 2), width // 2)
+    def y_columns(c):
+        t, kind = c
+        return pl.ds(pl.multiple_of((t * PERIOD + kind) * WIDTH, 128), PATTERN[kind][0])
+
+    def z_columns(c):
+        t, kind = c
+        return pl.ds(pl.multiple_of((t * PERIOD + kind) * WIDTH + PATTERN[kind][0], 128), PATTERN[kind][1])
+
+    def far_columns(c):
+        t, kind = c
+        return pl.ds(pl.multiple_of(t * Z_SPAN + sum(z for _, z in PATTERN[:kind]), 128), PATTERN[kind][1])
+
+    def index(c):
+        return c[0] * PERIOD + c[1]
 
     def added(*values):
         total = values[0].astype(jnp.float32)
@@ -228,82 +259,120 @@
             total = total + value.astype(jnp.float32)
         return total.astype(jnp.bfloat16)
 
-    above, below = device(y_of(1), z), device(y_of(NY - 1), z)
-    own, next_y, opposite, last_y = (pl.ds(block * i, block) for i in range(NY))
+    def rows_at(first, count):
+        return pl.ds(first * piece, count * piece)
+
+    y_above, y_below, y_across = (device(y_of(apart), z) for apart in (1, 3, 2))
+    z_above, z_below, z_across = (device(y, z_of[slot]) for slot in (1, 2, 3))
+    far_goes_down = z_lo < 2
+    far_passes = lax.rem(z_lo, 3) == 0
+
+    def multiply(c):
+        columns = pl.ds(pl.multiple_of(index(c) * WIDTH, 128), WIDTH)
+        start(c, jnp.dot(rot[...], levels[:, columns], preferred_element_type=jnp.float32))
+
+    def start(c, product):
+        columns = pl.ds(pl.multiple_of(index(c) * WIDTH, 128), WIDTH)
+        product = (product * scale[:, columns]).astype(jnp.bfloat16)
+        y_width = PATTERN[c[1]][0]
+        part[:, y_columns(c)] = product[:, :y_width]
+        for apart in range(NY):
+            for slot in range(4):
+                row = (apart * 4 + slot) * piece
+                part[rows_at(slot * NY + apart, 1), z_columns(c)] = product[row : row + piece, y_width:]
+
+        @pl.when(far_goes_down)
+        def _():
+            send(part.at[rows_at(12, 4), z_columns(c)], far_above.at[:, far_columns(c)], a_send, a_recv.at[3, index(c)], z_below)
+
+        @pl.when(jnp.logical_not(far_goes_down))
+        def _():
+            send(part.at[rows_at(12, 4), z_columns(c)], far_below.at[:, far_columns(c)], a_send, a_recv.at[2, index(c)], z_above)
+
+        send(part.at[rows_at(8, 2), y_columns(c)], from_below_a.at[:, y_columns(c)], a_send, a_recv.at[0, index(c)], y_above)
+        send(part.at[rows_at(10, 2), y_columns(c)], from_above_a.at[:, y_columns(c)], a_send, a_recv.at[1, index(c)], y_below)
+
+    def pass_on(c):
+        @pl.when(far_passes)
+        def _():
+            wait_for(far_below.at[:, far_columns(c)], a_recv.at[2, index(c)])
+            part[rows_at(4, 4), z_columns(c)] = added(part[rows_at(4, 4), z_columns(c)], far_below[:, far_columns(c)])
+            wait_for(far_above.at[:, far_columns(c)], a_recv.at[3, index(c)])
+            part[rows_at(8, 4), z_columns(c)] = added(part[rows_at(8, 4), z_columns(c)], far_above[:, far_columns(c)])
+
+        send(part.at[rows_at(4, 4), z_columns(c)], from_below_b.at[:, z_columns(c)], b_send, b_recv.at[2, index(c)], z_above)
+        send(part.at[rows_at(8, 4), z_columns(c)], from_above_b.at[:, z_columns(c)], b_send, b_recv.at[3, index(c)], z_below)
+        wait_for(from_below_a.at[:, y_columns(c)], a_recv.at[0, index(c)])
+        part[rows_at(4, 2), y_columns(c)] = added(part[rows_at(4, 2), y_columns(c)], from_below_a[:, y_columns(c)])
+        send(part.at[rows_at(4, 4), y_columns(c)], from_below_b.at[:, y_columns(c)], b_send, b_recv.at[0, index(c)], y_above)
+        wait_for(from_above_a.at[:, y_columns(c)], a_recv.at[1, index(c)])
+        part[rows_at(14, 2), y_columns(c)] = added(part[rows_at(14, 2), y_columns(c)], from_above_a[:, y_columns(c)])
+        send(part.at[rows_at(12, 4), y_columns(c)], from_above_b.at[:, y_columns(c)], b_send, b_recv.at[1, index(c)], y_below)
+
+    def to_owners(c):
+        def summed(columns, low):
+            wait_for(from_below_b.at[:, columns], b_recv.at[low, index(c)])
+            wait_for(from_above_b.at[:, columns], b_recv.at[low + 1, index(c)])
+            part[rows_at(0, 4), columns] = added(
+                part[rows_at(0, 4), columns], from_below_b[:, columns], from_above_b[:, columns]
+            )
+
+        def give(row, place, columns, sem, where):
+            send(part.at[rows_at(row, 1), columns], from_owners.at[rows_at(place, 1), columns], c_send, c_recv.at[sem, index(c)], where)
+
+        summed(z_columns(c), 2)
+        give(2, 1, z_columns(c), 4, y_across)
+        give(1, 0, z_columns(c), 3, y_above)
+        give(3, 2, z_columns(c), 5, y_below)
+        summed(y_columns(c), 0)
+        give(3, 1, y_columns(c), 1, z_across)
+        give(1, 0, y_columns(c), 0, z_above)
+        give(2, 2, y_columns(c), 2, z_below)
+
+    def finish(c):
+        for columns, low in ((y_columns(c), 0), (z_columns(c), 3)):
+            for place in range(3):
+                wait_for(from_owners.at[rows_at(place, 1), columns], c_recv.at[low + place, index(c)])
+            out_ref[:, columns] = added(
+                part[rows_at(0, 1), columns], *(from_owners[rows_at(place, 1), columns] for place in range(3))
+            )
 
     def step(t, carry):
-        @pl.when(t < chunks)
-        def _():
-            c = t
-            product = jnp.dot(rot[...], levels[:, columns_of(c)], preferred_element_type=jnp.float32)
-            part[:, columns_of(c)] = (product * scale_ref[:, columns_of(c)]).astype(jnp.bfloat16)
-            send(part.at[opposite, lower_of(c)], from_below_a.at[:, half_of(c)], a_send, a_recv.at[0, c], above)
-            send(part.at[opposite, upper_of(c)], from_above_a.at[:, half_of(c)], a_send, a_recv.at[1, c], below)
-
-        @pl.when((t >= LAG_B) & (t < chunks + LAG_B))
-        def _():
-            c = t - LAG_B
-            wait_for(from_below_a.at[:, half_of(c)], a_recv.at[0, c])
-            part[next_y, lower_of(c)] = added(part[next_y, lower_of(c)], from_below_a[:, half_of(c)])
-            send(part.at[next_y, columns_of(c)], from_below_b.at[:, columns_of(c)], b_send, b_recv.at[0, c], above)
-            wait_for(from_above_a.at[:, half_of(c)], a_recv.at[1, c])
-            part[last_y, upper_of(c)] = added(part[last_y, upper_of(c)], from_above_a[:, half_of(c)])
-            send(part.at[last_y, columns_of(c)], from_above_b.at[:, columns_of(c)], b_send, b_recv.at[1, c], below)
-
-        @pl.when((t >= LAG_C) & (t < chunks + LAG_C))
-        def _():
-            c = t - LAG_C
-            wait_for(from_below_b.at[:, columns_of(c)], b_recv.at[0, c])
-            wait_for(from_above_b.at[:, columns_of(c)], b_recv.at[1, c])
-            part[own, columns_of(c)] = added(
-                part[own, columns_of(c)], from_below_b[:, columns_of(c)], from_above_b[:, columns_of(c)]
-            )
-            for slot in (3, 1, 2):
-                send(
-                    part.at[pl.ds(slot * piece, piece), columns_of(c)],
-                    from_z.at[pl.ds((slot_there[slot] - 1) * piece, piece), columns_of(c)],
-                    z_send,
-                    z_recv.at[slot_there[slot] - 1, c],
-                    device(y, z_of[slot]),
-                )
-
-        @pl.when(t >= LAG_D)
-        def _():
-            c = t - LAG_D
-            for slot in range(3):
-                wait_for(from_z.at[pl.ds(slot * piece, piece), columns_of(c)], z_recv.at[slot, c])
-            out_ref[:, columns_of(c)] = added(
-                part[pl.ds(0, piece), columns_of(c)],
-                *(from_z[pl.ds(slot * piece, piece), columns_of(c)] for slot in range(3)),
-            )
-
+        for kind in range(PERIOD):
+            for lag, work in ((0, multiply), (LAG_B, pass_on), (LAG_C, to_owners), (LAG_D, finish)):
+                chunk = (t + (kind - lag) // PERIOD, (kind - lag) % PERIOD)
+                at = index(chunk)
+                lowest = FIRST if lag == 0 else 0
+                pl.when((at >= lowest) & (at < chunks))(functools.partial(work, chunk))
         return carry
 
-    lax.fori_loop(0, chunks + LAG_D, step, 0)
+    for kind in range(FIRST):
+        start((0, kind), first[:, kind * WIDTH : (kind + 1) * WIDTH])
+    lax.fori_loop(0, (chunks + LAG_D + PERIOD - 1) // PERIOD, step, 0)
 
     wait_for(gathered.at[pl.ds(0, (SHARDS - 1) * piece), :], gather_send)
     wait_for(rot.at[pl.ds(0, (SHARDS - 1) * piece), :], scatter_send)
-    wait_for(part.at[opposite, :], a_send)
-    wait_for(part.at[pl.ds(0, 2 * block), :], b_send)
-    wait_for(from_z, z_send)
+    wait_for(part.at[rows_at(0, 4), :], a_send)
+    wait_for(part.at[rows_at(0, 8), :], b_send)
+    wait_for(from_owners, c_send)
 
 
 def body(gate_inputs, up_inputs, down_codes, column_scale, half):
     rows, hidden_width = gate_inputs.shape
     code_rows, features = down_codes.shape
-    width = min(512, features // 2)
-    chunks = features // width
+    chunks = features // WIDTH
     supers = hidden_width // SUPER
     piece, block = rows // SHARDS, rows // NY
-    whole = pl.BlockSpec(memory_space=pltpu.VMEM)
     outside = pl.BlockSpec(memory_space=pl.ANY)
     b16 = jnp.bfloat16
     return pl.pallas_call(
-        functools.partial(kernel, half, width),
+        functools.partial(kernel, half),
         out_shape=jax.ShapeDtypeStruct((piece, features), b16),
-        in_specs=[outside, outside, outside, whole, whole],
-        out_specs=whole,
+        in_specs=[outside] * 5,
+        out_specs=pl.BlockSpec(memory_space=pltpu.VMEM),
         scratch_shapes=[
+            pltpu.VMEM((1, features), jnp.float32),
+            pltpu.VMEM((SUPER, SUPER), b16),
             pltpu.VMEM((rows, hidden_width), b16),
             pltpu.VMEM((rows, hidden_width), b16),
             pltpu.VMEM((code_rows, features), jnp.float32),
@@ -312,24 +381,27 @@
             pltpu.VMEM((rows, hidden_width), b16),
             pltpu.VMEM((rows, hidden_width), b16),
             pltpu.VMEM((hidden_width, features), b16),
+            pltpu.VMEM((rows, FIRST * WIDTH), jnp.float32),
             pltpu.VMEM((rows, features), b16),
-            pltpu.VMEM((block, features // 2), b16),
-            pltpu.VMEM((block, features // 2), b16),
+            pltpu.VMEM((block // 2, features), b16),
+            pltpu.VMEM((block // 2, features), b16),
+            pltpu.VMEM((block, chunks // PERIOD * Z_SPAN), b16),
+            pltpu.VMEM((block, chunks // PERIOD * Z_SPAN), b16),
             pltpu.VMEM((block, features), b16),
             pltpu.VMEM((block, features), b16),
             pltpu.VMEM((3 * piece, features), b16),
-            pltpu.SemaphoreType.DMA((2,)),
+            pltpu.SemaphoreType.DMA((3, supers)),
             pltpu.SemaphoreType.DMA((supers,)),
             pltpu.SemaphoreType.DMA,
             pltpu.SemaphoreType.DMA((supers,)),
             pltpu.SemaphoreType.DMA,
             pltpu.SemaphoreType.DMA((supers,)),
             pltpu.SemaphoreType.DMA,
-            pltpu.SemaphoreType.DMA((2, chunks)),
+            pltpu.SemaphoreType.DMA((4, chunks)),
             pltpu.SemaphoreType.DMA,
-            pltpu.SemaphoreType.DMA((2, chunks)),
+            pltpu.SemaphoreType.DMA((4, chunks)),
             pltpu.SemaphoreType.DMA,
-            pltpu.SemaphoreType.DMA((3, chunks)),
+            pltpu.SemaphoreType.DMA((6, chunks)),
         ],
         compiler_params=pltpu.CompilerParams(
             collective_id=0, has_side_effects=True, vmem_limit_bytes=60 * 1024 * 1024

time: 85.7 us -> 77.7 us (0.907)
  Pallas kernels: 83.8 us -> 75.9 us
    pallas_call x1, Pallas kernels: 83.8 us -> 75.9 us  [body(): pl.pallas_call(functools.partial(kernel, half), out_shape=jax.ShapeDtypeS...]
where the time goes in v2:
time: 77.7 us; the launch traced here: 77.6 us
  Pallas kernels  75.9 us (98%)
  local copies, waits for them, and re-layouts  1.67 us (2%)
    pallas_call x1, Pallas kernels, body(): pl.pallas_call(functools.partial(kernel, half), out_shape=jax.ShapeDtypeS...  75.9 us
    unnamed x1, local copies, waits for them, and re-layouts  1.67 us

profile of v2, /device:TPU:4, one launch (start us, length us, event | category | flops | bytes accessed | tf_op | source)
XLA Modules:
  0.0 77.6 jit_solution(6851461581609004355)
XLA Ops:
  0.0 75.9 %shard_map.55 = bf16[16,8192]{1,0:T(8,128)(2,1)} custom-call(bf16[256,1920]{1,0:T(8,128)(2,1)} %gate_hbm.1, bf16[256,1920]{1,0:T(8,128)(2,1)} %up_hbm.1, f32[320,8192]{1,0:T(8,128)} %codes_hbm.1, f32[1,8192]{1,0:T(1,128)} %bitcast.1, bf16[384,384]{1,0:T(8,128)(2,1)} %constant.2.clone.turn_hbm), custom_call_target="tpu_custom_call" | custom-call | tf_op jit(solution)/shard_map/pallas_call | solution.py:368
  75.9 1.7 %copy.7 = bf16[16,8192]{1,0:T(8,128)(2,1)} copy(bf16[16,8192]{1,0:T(8,128)(2,1)} %shard_map.55) | data formatting | bytes 524288

commit v3 on v2

--- a/solution.py
+++ b/solution.py
@@ -15,12 +15,13 @@
 SHARDS = NY * RUN
 SUPER = 384
 CODE_ROWS = SUPER // 6
-PATTERN = ((384, 128), (384, 128), (384, 128), (256, 256))
+PATTERN = ((384, 128), (256, 256))
 PERIOD = len(PATTERN)
 WIDTH = sum(PATTERN[0])
+DIRECT = 4
 FIRST = 2
 Z_SPAN = sum(z_width for _, z_width in PATTERN)
-LAG_B, LAG_C, LAG_D = 6, 10, 14
+LAGS = 4, 8, 12, 16
 
 
 def sylvester(extent):
@@ -64,7 +65,9 @@
     far_above,
     from_below_b,
     from_above_b,
-    from_owners,
+    from_below_c,
+    from_above_c,
+    from_next,
     load_sem,
     code_sem,
     gather_send,
@@ -77,6 +80,9 @@
     b_recv,
     c_send,
     c_recv,
+    d_send,
+    e_send,
+    d_recv,
 ):
     rows, hidden_width = gate.shape
     features = levels.shape[1]
@@ -253,6 +259,8 @@
     def index(c):
         return c[0] * PERIOD + c[1]
 
+    shared_chunks = max(chunks - DIRECT, 0)
+
     def added(*values):
         total = values[0].astype(jnp.float32)
         for value in values[1:]:
@@ -317,44 +325,109 @@
                 part[rows_at(0, 4), columns], from_below_b[:, columns], from_above_b[:, columns]
             )
 
-        def give(row, place, columns, sem, where):
-            send(part.at[rows_at(row, 1), columns], from_owners.at[rows_at(place, 1), columns], c_send, c_recv.at[sem, index(c)], where)
-
+        def give(row, buffer, columns, sem, where):
+            send(part.at[rows_at(row, 1), columns], buffer.at[:, columns], c_send, c_recv.at[sem, index(c)], where)
+
+        shared = index(c) < shared_chunks
         summed(z_columns(c), 2)
-        give(2, 1, z_columns(c), 4, y_across)
-        give(1, 0, z_columns(c), 3, y_above)
-        give(3, 2, z_columns(c), 5, y_below)
+
+        @pl.when(shared)
+        def _():
+            if c[1] % 2 == 0:
+                give(2, from_below_c, z_columns(c), 2, y_above)
+            else:
+                give(2, from_above_c, z_columns(c), 2, y_below)
+
+        @pl.when(jnp.logical_not(shared))
+        def _():
+            give_last(c, 2, 2, z_columns(c), 5, y_across, e_send)
+            give_last(c, 1, 0, z_columns(c), 2, y_above, e_send)
+            give_last(c, 3, 1, z_columns(c), 3, y_below, e_send)
+
         summed(y_columns(c), 0)
-        give(3, 1, y_columns(c), 1, z_across)
-        give(1, 0, y_columns(c), 0, z_above)
-        give(2, 2, y_columns(c), 2, z_below)
+
+        @pl.when(shared)
+        def _():
+            pl.when(far_goes_down)(lambda: give(3, from_above_c, y_columns(c), 1, z_below))
+            pl.when(jnp.logical_not(far_goes_down))(lambda: give(3, from_below_c, y_columns(c), 0, z_above))
+
+        @pl.when(jnp.logical_not(shared))
+        def _():
+            give_last(c, 3, 2, y_columns(c), 4, z_across, e_send)
+            give_last(c, 1, 0, y_columns(c), 0, z_above, e_send)
+            give_last(c, 2, 1, y_columns(c), 1, z_below, e_send)
+
+    def give_last(c, row, place, columns, sem, where, done):
+        send(
+            part.at[rows_at(row, 1), columns],
+            from_next.at[rows_at(place, 1), columns],
+            done,
+            d_recv.at[sem, index(c)],
+            where,
+        )
+
+    def last_hop(c):
+        def add(row, buffer, columns, sem):
+            wait_for(buffer.at[:, columns], c_recv.at[sem, index(c)])
+            part[rows_at(row, 1), columns] = added(part[rows_at(row, 1), columns], buffer[:, columns])
+
+        if c[1] % 2 == 0:
+            add(1, from_below_c, z_columns(c), 2)
+        else:
+            add(3, from_above_c, z_columns(c), 2)
+        give_last(c, 1, 0, z_columns(c), 2, y_above, d_send)
+        give_last(c, 3, 1, z_columns(c), 3, y_below, d_send)
+
+        @pl.when(far_passes)
+        def _():
+            add(1, from_below_c, y_columns(c), 0)
+            add(2, from_above_c, y_columns(c), 1)
+
+        give_last(c, 1, 0, y_columns(c), 0, z_above, d_send)
+        give_last(c, 2, 1, y_columns(c), 1, z_below, d_send)
 
     def finish(c):
-        for columns, low in ((y_columns(c), 0), (z_columns(c), 3)):
-            for place in range(3):
-                wait_for(from_owners.at[rows_at(place, 1), columns], c_recv.at[low + place, index(c)])
+        def total(columns, sems):
+            for place, sem in enumerate(sems):
+                wait_for(from_next.at[rows_at(place, 1), columns], d_recv.at[sem, index(c)])
             out_ref[:, columns] = added(
-                part[rows_at(0, 1), columns], *(from_owners[rows_at(place, 1), columns] for place in range(3))
+                part[rows_at(0, 1), columns], *(from_next[rows_at(place, 1), columns] for place in range(len(sems)))
             )
+
+        @pl.when(index(c) < shared_chunks)
+        def _():
+            total(y_columns(c), (0, 1))
+            total(z_columns(c), (2, 3))
+
+        @pl.when(index(c) >= shared_chunks)
+        def _():
+            total(y_columns(c), (0, 1, 4))
+            total(z_columns(c), (2, 3, 5))
 
     def step(t, carry):
         for kind in range(PERIOD):
-            for lag, work in ((0, multiply), (LAG_B, pass_on), (LAG_C, to_owners), (LAG_D, finish)):
+            for lag, work in zip((0, *LAGS), (multiply, pass_on, to_owners, last_hop, finish)):
                 chunk = (t + (kind - lag) // PERIOD, (kind - lag) % PERIOD)
                 at = index(chunk)
                 lowest = FIRST if lag == 0 else 0
-                pl.when((at >= lowest) & (at < chunks))(functools.partial(work, chunk))
+                highest = shared_chunks if work is last_hop else chunks
+                pl.when((at >= lowest) & (at < highest))(functools.partial(work, chunk))
         return carry
 
     for kind in range(FIRST):
         start((0, kind), first[:, kind * WIDTH : (kind + 1) * WIDTH])
-    lax.fori_loop(0, (chunks + LAG_D + PERIOD - 1) // PERIOD, step, 0)
+    lax.fori_loop(0, (chunks + LAGS[-1] + PERIOD - 1) // PERIOD, step, 0)
 
     wait_for(gathered.at[pl.ds(0, (SHARDS - 1) * piece), :], gather_send)
     wait_for(rot.at[pl.ds(0, (SHARDS - 1) * piece), :], scatter_send)
     wait_for(part.at[rows_at(0, 4), :], a_send)
     wait_for(part.at[rows_at(0, 8), :], b_send)
-    wait_for(from_owners, c_send)
+    split = shared_chunks * WIDTH
+    if split:
+        wait_for(part.at[rows_at(0, 1), 0:split], c_send)
+        wait_for(from_next.at[rows_at(0, 2), 0:split], d_send)
+    if split < features:
+        wait_for(from_next.at[:, split:features], e_send)
 
 
 def body(gate_inputs, up_inputs, down_codes, column_scale, half):
@@ -389,6 +462,8 @@
             pltpu.VMEM((block, chunks // PERIOD * Z_SPAN), b16),
             pltpu.VMEM((block, features), b16),
             pltpu.VMEM((block, features), b16),
+            pltpu.VMEM((piece, features), b16),
+            pltpu.VMEM((piece, features), b16),
             pltpu.VMEM((3 * piece, features), b16),
             pltpu.SemaphoreType.DMA((3, supers)),
             pltpu.SemaphoreType.DMA((supers,)),
@@ -400,6 +475,9 @@
             pltpu.SemaphoreType.DMA((4, chunks)),
             pltpu.SemaphoreType.DMA,
             pltpu.SemaphoreType.DMA((4, chunks)),
+            pltpu.SemaphoreType.DMA,
+            pltpu.SemaphoreType.DMA((3, chunks)),
+            pltpu.SemaphoreType.DMA,
             pltpu.SemaphoreType.DMA,
             pltpu.SemaphoreType.DMA((6, chunks)),
         ],

time: 77.7 us -> 75.2 us (0.968)
  Pallas kernels: 75.9 us -> 73.4 us
    pallas_call x1, Pallas kernels: 75.9 us -> 73.4 us  [body(): pl.pallas_call(functools.partial(kernel, half), out_shape=jax.ShapeDtypeS...]
where the time goes in v3:
time: 75.2 us; the launch traced here: 75.1 us
  Pallas kernels  73.4 us (98%)
  local copies, waits for them, and re-layouts  1.67 us (2%)
    pallas_call x1, Pallas kernels, body(): pl.pallas_call(functools.partial(kernel, half), out_shape=jax.ShapeDtypeS...  73.4 us
    unnamed x1, local copies, waits for them, and re-layouts  1.67 us

profile of v3, /device:TPU:4, one launch (start us, length us, event | category | flops | bytes accessed | tf_op | source)
XLA Modules:
  0.0 75.1 jit_solution(1792533444547680317)
XLA Ops:
  0.0 73.4 %shard_map.55 = bf16[16,8192]{1,0:T(8,128)(2,1)} custom-call(bf16[256,1920]{1,0:T(8,128)(2,1)} %gate_hbm.1, bf16[256,1920]{1,0:T(8,128)(2,1)} %up_hbm.1, f32[320,8192]{1,0:T(8,128)} %codes_hbm.1, f32[1,8192]{1,0:T(1,128)} %bitcast.1, bf16[384,384]{1,0:T(8,128)(2,1)} %constant.2.clone.turn_hbm), custom_call_target="tpu_custom_call" | custom-call | tf_op jit(solution)/shard_map/pallas_call | solution.py:441
  73.5 1.7 %copy.7 = bf16[16,8192]{1,0:T(8,128)(2,1)} copy(bf16[16,8192]{1,0:T(8,128)(2,1)} %shard_map.55) | data formatting | bytes 524288

commit v4 on v3

--- a/solution.py
+++ b/solution.py
@@ -18,10 +18,10 @@
 PATTERN = ((384, 128), (256, 256))
 PERIOD = len(PATTERN)
 WIDTH = sum(PATTERN[0])
-DIRECT = 4
-FIRST = 2
+DIRECT = 6
+FIRST = 4
 Z_SPAN = sum(z_width for _, z_width in PATTERN)
-LAGS = 4, 8, 12, 16
+LAGS = 5, 9, 13, 17
 
 
 def sylvester(extent):
@@ -46,7 +46,8 @@
     codes_hbm,
     scale_hbm,
     turn_hbm,
-    out_ref,
+    out_hbm,
+    out,
     scale,
     turn,
     gate,
@@ -68,6 +69,7 @@
     from_below_c,
     from_above_c,
     from_next,
+    out_sem,
     load_sem,
     code_sem,
     gather_send,
@@ -119,6 +121,19 @@
         pl.semaphore_signal(barrier, inc=1, device_id=(dp, lax.rem(me + apart, SHARDS)), device_id_type=MESH)
         return carry
 
+    lax.fori_loop(1, SHARDS, greet, 0)
+    for slot in (1, 2, 3):
+
+        @pl.when(lax.div(z_of[slot], RUN) != lax.div(z, RUN))
+        def _(slot=slot):
+            def greet_across(apart, carry):
+                pl.semaphore_signal(
+                    barrier, inc=1, device_id=device(y_of(apart), z_of[slot]), device_id_type=MESH
+                )
+                return carry
+
+            lax.fori_loop(0, NY, greet_across, 0)
+
     def input_copies(q):
         span = pl.ds(pl.multiple_of(q * SUPER, 128), SUPER)
         return (
@@ -133,19 +148,6 @@
     load_scale = pltpu.make_async_copy(scale_hbm, scale, load_sem.at[2, 1])
     load_turn.start()
     load_scale.start()
-    lax.fori_loop(1, SHARDS, greet, 0)
-    for slot in (1, 2, 3):
-
-        @pl.when(lax.div(z_of[slot], RUN) != lax.div(z, RUN))
-        def _(slot=slot):
-            def greet_across(apart, carry):
-                pl.semaphore_signal(
-                    barrier, inc=1, device_id=device(y_of(apart), z_of[slot]), device_id_type=MESH
-                )
-                return carry
-
-            lax.fori_loop(0, NY, greet_across, 0)
-
     def code_copy(q):
         span = pl.ds(pl.multiple_of(q * CODE_ROWS, CODE_ROWS), CODE_ROWS)
         return pltpu.make_async_copy(codes_hbm.at[span, :], codes.at[span, :], code_sem.at[q])
@@ -233,16 +235,21 @@
     lax.fori_loop(0, supers, rotate, 0)
     decode_levels(supers - 1)
 
-    def wait_rotated(q, carry):
+    def wait_rotated(q):
         span = pl.ds(pl.multiple_of(q * SUPER, 128), SUPER)
         wait_for(rot.at[pl.ds(0, (SHARDS - 1) * piece), span], scatter_recv.at[q])
+        return span
+
+    def grow(q, carry):
+        span = wait_rotated(q)
         first[...] += jnp.dot(
             rot[:, span], levels[span, 0 : FIRST * WIDTH], preferred_element_type=jnp.float32
         )
         return carry
 
     first[...] = jnp.zeros_like(first)
-    lax.fori_loop(0, supers, wait_rotated, 0)
+    lax.fori_loop(0, supers - 1, grow, 0)
+    last_span = wait_rotated(supers - 1)
 
     def y_columns(c):
         t, kind = c
@@ -390,7 +397,7 @@
         def total(columns, sems):
             for place, sem in enumerate(sems):
                 wait_for(from_next.at[rows_at(place, 1), columns], d_recv.at[sem, index(c)])
-            out_ref[:, columns] = added(
+            out[:, columns] = added(
                 part[rows_at(0, 1), columns], *(from_next[rows_at(place, 1), columns] for place in range(len(sems)))
             )
 
@@ -404,9 +411,12 @@
             total(y_columns(c), (0, 1, 4))
             total(z_columns(c), (2, 3, 5))
 
+        columns = pl.ds(pl.multiple_of(index(c) * WIDTH, 128), WIDTH)
+        pltpu.make_async_copy(out.at[:, columns], out_hbm.at[:, columns], out_sem).start()
+
     def step(t, carry):
         for kind in range(PERIOD):
-            for lag, work in zip((0, *LAGS), (multiply, pass_on, to_owners, last_hop, finish)):
+            for lag, work in zip((*LAGS, 0), (pass_on, to_owners, last_hop, finish, multiply)):
                 chunk = (t + (kind - lag) // PERIOD, (kind - lag) % PERIOD)
                 at = index(chunk)
                 lowest = FIRST if lag == 0 else 0
@@ -415,9 +425,12 @@
         return carry
 
     for kind in range(FIRST):
-        start((0, kind), first[:, kind * WIDTH : (kind + 1) * WIDTH])
+        columns = slice(kind * WIDTH, (kind + 1) * WIDTH)
+        product = jnp.dot(rot[:, last_span], levels[last_span, columns], preferred_element_type=jnp.float32)
+        start((kind // PERIOD, kind % PERIOD), first[:, columns] + product)
     lax.fori_loop(0, (chunks + LAGS[-1] + PERIOD - 1) // PERIOD, step, 0)
 
+    wait_for(out, out_sem)
     wait_for(gathered.at[pl.ds(0, (SHARDS - 1) * piece), :], gather_send)
     wait_for(rot.at[pl.ds(0, (SHARDS - 1) * piece), :], scatter_send)
     wait_for(part.at[rows_at(0, 4), :], a_send)
@@ -442,8 +455,9 @@
         functools.partial(kernel, half),
         out_shape=jax.ShapeDtypeStruct((piece, features), b16),
         in_specs=[outside] * 5,
-        out_specs=pl.BlockSpec(memory_space=pltpu.VMEM),
+        out_specs=outside,
         scratch_shapes=[
+            pltpu.VMEM((piece, features), b16),
             pltpu.VMEM((1, features), jnp.float32),
             pltpu.VMEM((SUPER, SUPER), b16),
             pltpu.VMEM((rows, hidden_width), b16),
@@ -465,6 +479,7 @@
             pltpu.VMEM((piece, features), b16),
             pltpu.VMEM((piece, features), b16),
             pltpu.VMEM((3 * piece, features), b16),
+            pltpu.SemaphoreType.DMA,
             pltpu.SemaphoreType.DMA((3, supers)),
             pltpu.SemaphoreType.DMA((supers,)),
             pltpu.SemaphoreType.DMA,

time: 75.2 us -> 74.7 us (level)
  no operation moved by 1% of the time
where the time goes in v4:
time: 74.7 us; the launch traced here: 74.6 us
  Pallas kernels  72.9 us (98%)
  local copies, waits for them, and re-layouts  1.67 us (2%)
    pallas_call x1, Pallas kernels, body(): pl.pallas_call(functools.partial(kernel, half), out_shape=jax.ShapeDtypeS...  72.9 us
    unnamed x1, local copies, waits for them, and re-layouts  1.67 us

profile of v4, /device:TPU:4, one launch (start us, length us, event | category | flops | bytes accessed | tf_op | source)
XLA Modules:
  0.0 74.6 jit_solution(4615441141251628395)
XLA Ops:
  0.0 72.9 %shard_map.55 = bf16[16,8192]{1,0:T(8,128)(2,1)} custom-call(bf16[256,1920]{1,0:T(8,128)(2,1)} %gate_hbm.1, bf16[256,1920]{1,0:T(8,128)(2,1)} %up_hbm.1, f32[320,8192]{1,0:T(8,128)} %codes_hbm.1, f32[1,8192]{1,0:T(1,128)} %bitcast.1, bf16[384,384]{1,0:T(8,128)(2,1)} %constant.2.clone.turn_hbm), custom_call_target="tpu_custom_call" | custom-call | tf_op jit(solution)/shard_map/pallas_call | solution.py:454
  72.9 1.7 %copy.7 = bf16[16,8192]{1,0:T(8,128)(2,1)} copy(bf16[16,8192]{1,0:T(8,128)(2,1)} %shard_map.55) | data formatting | bytes 524288

commit v5 on v4

--- a/solution.py
+++ b/solution.py
@@ -153,6 +153,8 @@
         return pltpu.make_async_copy(codes_hbm.at[span, :], codes.at[span, :], code_sem.at[q])
 
     across = 1 + lax.rem(lax.div(z_lo + 1, 2) + 1, 2)
+    for q in range(supers):
+        code_copy(q).start()
     pl.semaphore_wait(barrier, SHARDS - 1 + NY * across)
 
     def send_hidden(q, carry):
@@ -179,8 +181,6 @@
         return carry
 
     lax.fori_loop(0, supers, send_hidden, 0)
-    for q in range(supers):
-        code_copy(q).start()
     load_turn.wait()
     load_scale.wait()
 
@@ -308,21 +308,22 @@
         send(part.at[rows_at(10, 2), y_columns(c)], from_above_a.at[:, y_columns(c)], a_send, a_recv.at[1, index(c)], y_below)
 
     def pass_on(c):
-        @pl.when(far_passes)
-        def _():
-            wait_for(far_below.at[:, far_columns(c)], a_recv.at[2, index(c)])
-            part[rows_at(4, 4), z_columns(c)] = added(part[rows_at(4, 4), z_columns(c)], far_below[:, far_columns(c)])
-            wait_for(far_above.at[:, far_columns(c)], a_recv.at[3, index(c)])
-            part[rows_at(8, 4), z_columns(c)] = added(part[rows_at(8, 4), z_columns(c)], far_above[:, far_columns(c)])
-
-        send(part.at[rows_at(4, 4), z_columns(c)], from_below_b.at[:, z_columns(c)], b_send, b_recv.at[2, index(c)], z_above)
-        send(part.at[rows_at(8, 4), z_columns(c)], from_above_b.at[:, z_columns(c)], b_send, b_recv.at[3, index(c)], z_below)
         wait_for(from_below_a.at[:, y_columns(c)], a_recv.at[0, index(c)])
         part[rows_at(4, 2), y_columns(c)] = added(part[rows_at(4, 2), y_columns(c)], from_below_a[:, y_columns(c)])
         send(part.at[rows_at(4, 4), y_columns(c)], from_below_b.at[:, y_columns(c)], b_send, b_recv.at[0, index(c)], y_above)
         wait_for(from_above_a.at[:, y_columns(c)], a_recv.at[1, index(c)])
         part[rows_at(14, 2), y_columns(c)] = added(part[rows_at(14, 2), y_columns(c)], from_above_a[:, y_columns(c)])
         send(part.at[rows_at(12, 4), y_columns(c)], from_above_b.at[:, y_columns(c)], b_send, b_recv.at[1, index(c)], y_below)
+
+        @pl.when(far_passes)
+        def _():
+            wait_for(far_below.at[:, far_columns(c)], a_recv.at[2, index(c)])
+            part[rows_at(4, 4), z_columns(c)] = added(part[rows_at(4, 4), z_columns(c)], far_below[:, far_columns(c)])
+            wait_for(far_above.at[:, far_columns(c)], a_recv.at[3, index(c)])
+            part[rows_at(8, 4), z_columns(c)] = added(part[rows_at(8, 4), z_columns(c)], far_above[:, far_columns(c)])
+
+        send(part.at[rows_at(4, 4), z_columns(c)], from_below_b.at[:, z_columns(c)], b_send, b_recv.at[2, index(c)], z_above)
+        send(part.at[rows_at(8, 4), z_columns(c)], from_above_b.at[:, z_columns(c)], b_send, b_recv.at[3, index(c)], z_below)
 
     def to_owners(c):
         def summed(columns, low):

time: 74.7 us -> 74.5 us (level)
  no operation moved by 1% of the time
where the time goes in v5:
time: 74.5 us; the launch traced here: 74.4 us
  Pallas kernels  72.7 us (98%)
  local copies, waits for them, and re-layouts  1.67 us (2%)
    pallas_call x1, Pallas kernels, body(): pl.pallas_call(functools.partial(kernel, half), out_shape=jax.ShapeDtypeS...  72.7 us
    unnamed x1, local copies, waits for them, and re-layouts  1.67 us

profile of v5, /device:TPU:4, one launch (start us, length us, event | category | flops | bytes accessed | tf_op | source)
XLA Modules:
  0.0 74.4 jit_solution(1314010249659826238)
XLA Ops:
  0.0 72.7 %shard_map.55 = bf16[16,8192]{1,0:T(8,128)(2,1)} custom-call(bf16[256,1920]{1,0:T(8,128)(2,1)} %gate_hbm.1, bf16[256,1920]{1,0:T(8,128)(2,1)} %up_hbm.1, f32[320,8192]{1,0:T(8,128)} %codes_hbm.1, f32[1,8192]{1,0:T(1,128)} %bitcast.1, bf16[384,384]{1,0:T(8,128)(2,1)} %constant.2.clone.turn_hbm), custom_call_target="tpu_custom_call" | custom-call | tf_op jit(solution)/shard_map/pallas_call | solution.py:455
  72.7 1.7 %copy.7 = bf16[16,8192]{1,0:T(8,128)(2,1)} copy(bf16[16,8192]{1,0:T(8,128)(2,1)} %shard_map.55) | data formatting | bytes 524288

commit v6 on v5

--- a/solution.py
+++ b/solution.py
@@ -296,16 +296,16 @@
                 row = (apart * 4 + slot) * piece
                 part[rows_at(slot * NY + apart, 1), z_columns(c)] = product[row : row + piece, y_width:]
 
-        @pl.when(far_goes_down)
-        def _():
-            send(part.at[rows_at(12, 4), z_columns(c)], far_above.at[:, far_columns(c)], a_send, a_recv.at[3, index(c)], z_below)
-
-        @pl.when(jnp.logical_not(far_goes_down))
-        def _():
-            send(part.at[rows_at(12, 4), z_columns(c)], far_below.at[:, far_columns(c)], a_send, a_recv.at[2, index(c)], z_above)
-
         send(part.at[rows_at(8, 2), y_columns(c)], from_below_a.at[:, y_columns(c)], a_send, a_recv.at[0, index(c)], y_above)
         send(part.at[rows_at(10, 2), y_columns(c)], from_above_a.at[:, y_columns(c)], a_send, a_recv.at[1, index(c)], y_below)
+
+        @pl.when(far_goes_down)
+        def _():
+            send(part.at[rows_at(12, 4), z_columns(c)], far_above.at[:, far_columns(c)], a_send, a_recv.at[3, index(c)], z_below)
+
+        @pl.when(jnp.logical_not(far_goes_down))
+        def _():
+            send(part.at[rows_at(12, 4), z_columns(c)], far_below.at[:, far_columns(c)], a_send, a_recv.at[2, index(c)], z_above)
 
     def pass_on(c):
         wait_for(from_below_a.at[:, y_columns(c)], a_recv.at[0, index(c)])

time: 74.5 us -> 74.5 us (level)
  no operation moved by 1% of the time
where the time goes in v6:
time: 74.5 us; the launch traced here: 74.4 us
  Pallas kernels  72.7 us (98%)
  local copies, waits for them, and re-layouts  1.67 us (2%)
    pallas_call x1, Pallas kernels, body(): pl.pallas_call(functools.partial(kernel, half), out_shape=jax.ShapeDtypeS...  72.7 us
    unnamed x1, local copies, waits for them, and re-layouts  1.67 us

profile of v6, /device:TPU:4, one launch (start us, length us, event | category | flops | bytes accessed | tf_op | source)
XLA Modules:
  0.0 74.4 jit_solution(17843526717685442335)
XLA Ops:
  0.0 72.7 %shard_map.55 = bf16[16,8192]{1,0:T(8,128)(2,1)} custom-call(bf16[256,1920]{1,0:T(8,128)(2,1)} %gate_hbm.1, bf16[256,1920]{1,0:T(8,128)(2,1)} %up_hbm.1, f32[320,8192]{1,0:T(8,128)} %codes_hbm.1, f32[1,8192]{1,0:T(1,128)} %bitcast.1, bf16[384,384]{1,0:T(8,128)(2,1)} %constant.2.clone.turn_hbm), custom_call_target="tpu_custom_call" | custom-call | tf_op jit(solution)/shard_map/pallas_call | solution.py:455
  72.7 1.7 %copy.7 = bf16[16,8192]{1,0:T(8,128)(2,1)} copy(bf16[16,8192]{1,0:T(8,128)(2,1)} %shard_map.55) | data formatting | bytes 524288
